TPU v7x, 32 devices: a whole 2x2x4 slice. The times are simulated.
32 devices in a mesh: grp: 2 (over y), src: 16 (over z, x, core).
Axes of the slice: x: 2, y: 2, z: 4, core: 2. Of those that a mesh axis runs over, the one named last changes fastest.
Arguments:
- kernel: bfloat16 [2560, 256, 256], P(('grp', 'src')), parts along dimension 0, may hold values from 1.953125e-07 to 0.0146484375
- pair_source: int32 [2560], P(('grp', 'src')), parts along dimension 0, may hold values from 0 to 15, as said below
- pair_target: int32 [2560], P(('grp', 'src')), parts along dimension 0, may hold values from 0 to 21, as said below
- source_cells: int32 [512], P(('grp', 'src')), parts along dimension 0, may hold values from 129 to 256
- target_cells: int32 [512], P(('grp', 'src')), parts along dimension 0, may hold values from 129 to 256
- source_hist: bfloat16 [64, 131072], P(None, ('grp', 'src')), parts along dimension 1, may hold values from 0.049804688 to 2
- target_hist: bfloat16 [64, 131072], P(None, ('grp', 'src')), parts along dimension 1, may hold values from 0.05 to 2
- warm_start: bfloat16 [64, 131072], P(None, ('grp', 'src')), parts along dimension 1, may hold values from 0.5 to 2
Outputs:
- target_scaling: bfloat16 [64, 131072], P(None, ('grp', 'src')), parts along dimension 1
- row_marginal: bfloat16 [64, 131072], P(None, ('grp', 'src')), parts along dimension 1
There are 2 independent parts, one for each index of `grp`. A program takes and returns all parts, laid end to end along the dimension named above; each array names one. Nothing has to cross between parts.
Inputs may be any that keep to these rules, and one draw needn't show every extreme that they name: `pair_source`: on each device every source block has 1 to 7 pairs with distinct target positions, within 3 of its own index plus 3, always including that aligned position; on every device some source block has exactly 7 pairs. `pair_target`: window position w of a pair with source block b lies between b and b + 6.
All inputs are finite; a program needn't handle non-finite values.
Results may differ from a plain program's by a relative error of at most 0.008.
Values may be sent and summed in bfloat16 or wider, within the bound.
A program may use at most 64 MiB of HBM per device.

v0:
```python
import jax
import jax.numpy as jnp
from jax import lax
from jax.sharding import PartitionSpec as P

RIM = 3
ITERS = 2


def extended(block, sides, width):
    for axis, dim in sides:
        count = lax.axis_size(axis)
        forward = [(i, i + 1) for i in range(count - 1)]
        backward = [(target, source) for source, target in forward]
        low = lax.ppermute(
            lax.slice_in_dim(block, block.shape[dim] - width, None, axis=dim), axis, forward
        )
        high = lax.ppermute(lax.slice_in_dim(block, 0, width, axis=dim), axis, backward)
        block = jnp.concatenate([low, block, high], axis=dim)
    return block


def passed_along(block, axis, distance):
    devices = range(lax.axis_size(axis))
    route = [(i - distance, i) for i in devices if i - distance in devices]
    return lax.ppermute(block, axis, route)


def pair_total(product, selector, form):
    high_part = product.astype(jnp.bfloat16)
    low_part = (product - high_part.astype(jnp.float32)).astype(jnp.bfloat16)
    first = jnp.einsum(form, high_part, selector, preferred_element_type=jnp.float32)
    return first + jnp.einsum(form, low_part, selector, preferred_element_type=jnp.float32)


def local(
    kernel,
    pair_source,
    pair_target,
    source_cells,
    target_cells,
    source_hist,
    target_hist,
    warm_start,
):
    block_count = source_cells.shape[0]
    block_len = kernel.shape[1]
    hist_count = source_hist.shape[0]
    reach = RIM
    window_len = block_count + 2 * reach
    slot_ids = jnp.arange(block_len, dtype=jnp.int32)
    source_live = slot_ids[None, :] < source_cells[:, None]
    target_live = slot_ids[None, :] < target_cells[:, None]

    def masked(field, live):
        return jnp.where(
            live[None], field.reshape(hist_count, block_count, block_len).astype(jnp.float32), 0.0
        )

    source_mass = masked(source_hist, source_live)
    target_mass = masked(target_hist, target_live)
    scaling = masked(warm_start, target_live)
    source_pick = (
        pair_source[:, None] == jnp.arange(block_count, dtype=jnp.int32)[None, :]
    ).astype(jnp.bfloat16)
    window_pos = pair_target + (reach - RIM)
    target_pick = (window_pos[:, None] == jnp.arange(window_len, dtype=jnp.int32)[None, :]).astype(
        jnp.bfloat16
    )

    def forward(field):
        flat_scale = field.astype(jnp.bfloat16).reshape(hist_count, block_count * block_len)
        padded = extended(flat_scale, (("src", 1),), reach * block_len)
        window = padded.reshape(hist_count, window_len, block_len)
        picked = jnp.take(window, window_pos, axis=1)
        product = jnp.einsum("hpj,pij->hpi", picked, kernel, preferred_element_type=jnp.float32)
        return pair_total(product, source_pick, "hpi,ps->hsi")

    def backward(field):
        rounded = field.astype(jnp.bfloat16)
        picked = jnp.take(rounded, pair_source, axis=1)
        product = jnp.einsum("hpi,pij->hpj", picked, kernel, preferred_element_type=jnp.float32)
        partial_win = pair_total(product, target_pick, "hpj,pw->hwj")
        lower_part = partial_win[:, :reach]
        own_part = partial_win[:, reach : reach + block_count]
        upper_part = partial_win[:, reach + block_count :]
        from_upper = passed_along(lower_part.astype(jnp.bfloat16), "src", -1).astype(
            lower_part.dtype
        )
        from_lower = passed_along(upper_part.astype(jnp.bfloat16), "src", 1).astype(
            upper_part.dtype
        )
        own_part = own_part.at[:, block_count - reach :].add(from_upper)
        own_part = own_part.at[:, :reach].add(from_lower)
        return own_part

    source_scale = source_mass
    for sweep in range(ITERS):
        image = forward(scaling)
        source_scale = source_mass / image
        co_image = backward(source_scale)
        scaling = target_mass / co_image
    image = forward(scaling)
    marginal = source_scale * image
    total_len = block_count * block_len
    return (
        scaling.reshape(hist_count, total_len).astype(jnp.bfloat16),
        marginal.reshape(hist_count, total_len).astype(jnp.bfloat16),
    )


def solution(mesh):
    in_specs = (
        P(("grp", "src"), None, None),
        P(("grp", "src")),
        P(("grp", "src")),
        P(("grp", "src")),
        P(("grp", "src")),
        P(None, ("grp", "src")),
        P(None, ("grp", "src")),
        P(None, ("grp", "src")),
    )
    out_specs = (P(None, ("grp", "src")), P(None, ("grp", "src")))
    return jax.shard_map(local, mesh=mesh, in_specs=in_specs, out_specs=out_specs, check_vma=False)
```

profile of v0, /device:TPU:19, one launch (start us, length us, event | category | flops | bytes accessed | tf_op | source)
XLA Modules:
  0.0 123.2 jit_solution(3797362778570277245)
XLA Ops:
  0.7 0.7 lt.65
  1.4 1.1 select_convert_fusion
  2.6 3.7 %collective-permute-start = (bf16[64,768]{1,0:T(8,128)(2,1)S(1)}, bf16[64,768]{1,0:T(8,128)(2,1)S(1)}, u32[]{:S(2)}, u32[]{:S(2)}) collective-permute-start(bf16[64,768]{1,0:T(8,128)(2,1)S(1)} %get-tuple-element.70), channel_id=1, source_target_pairs={{0,1},{1,2},{2,3},{3,4},{4,5},{5,6},{6,7},{7,8},{8,9},{9,10},{10,1... | collective-permute-start | bytes 294920 | tf_op jit(solution)/shard_map/ppermute | solution.py:15
  6.3 1.9 %collective-permute-start.1 = (bf16[64,768]{1,0:T(8,128)(2,1)S(1)}, bf16[64,768]{1,0:T(8,128)(2,1)S(1)}, u32[]{:S(2)}, u32[]{:S(2)}) collective-permute-start(bf16[64,768]{1,0:T(8,128)(2,1)S(1)} %get-tuple-element.71), channel_id=1, source_target_pairs={{1,0},{2,1},{3,2},{4,3},{5,4},{6,5},{7,6},{8,7},{9,8},{10,9},{11,1... | collective-permute-start | bytes 294920 | tf_op jit(solution)/shard_map/ppermute | solution.py:18
  8.3 0.7 compare_and_fusion.1
  8.9 0.7 compare_select_fusion.1
  9.6 0.7 compare_and_fusion
  10.2 0.7 compare_select_fusion
  10.9 0.7 iota_compare_fusion
  11.6 1.2 copy.39
  12.8 1.1 bitcast_select_fusion
  14.1 0.8 gather_fusion
  14.8 8.8 %fusion.4 = (bf16[64,80,256]{2,0,1:T(8,128)(2,1)S(1)}, bf16[64,80,256]{2,0,1:T(8,128)(2,1)}) fusion(bf16[80,256,256]{2,1,0:T(8,128)(2,1)} %param.20, bf16[80,64,256]{2,1,0:T(8,128)(2,1)S(1)} %gather_fusion, pred[80]{0:T(512)(128)(4,1)S(1)} %compare_and_fusion.1), kind=kOutput, calls=%fused_computation.19 | convolution fusion | flops 677642240 | bytes 18350160 | tf_op jit(solution)/shard_map/hpj,pij->hpi/dot_general | solution.py:76
  23.6 1.5 %fusion.15 = f32[16,64,256]{2,0,1:T(8,128)S(1)} fusion(bf16[64,80,256]{2,0,1:T(8,128)(2,1)S(1)} %get-tuple-element.60, s32[80]{0:T(128)S(1)} %copy-done.10), kind=kOutput, calls=%fused_computation.30 | convolution fusion | flops 41944320 | bytes 3670336 | tf_op jit(solution)/shard_map/hpi,ps->hsi/dot_general | solution.py:33
  25.3 0.3 copy-done.5
  25.6 1.6 %fusion.81 = bf16[64,16,256]{2,1,0:T(8,128)(2,1)S(1)} fusion(f32[64,16,256]{2,1,0:T(8,128)S(1)} %copy-done.5, f32[16,64,256]{2,0,1:T(8,128)S(1)} %fusion.15, bf16[64,80,256]{2,0,1:T(8,128)(2,1)S(1)} %copy-done.4, s32[80]{0:T(128)S(1)} %copy-done.10), kind=kOutput, calls=%fused_computation.76 | convolution fusion | flops 42730752 | bytes 5243200 | tf_op jit(solution)/shard_map/hpi,ps->hsi/dot_general | solution.py:32
  27.4 0.7 gather_fusion.1
  28.1 6.0 %fusion.3 = (bf16[64,80,256]{2,0,1:T(8,128)(2,1)S(1)}, bf16[64,80,256]{2,0,1:T(8,128)(2,1)S(1)}) fusion(bf16[80,256,256]{2,1,0:T(8,128)(2,1)} %param.20, bf16[80,64,256]{2,1,0:T(8,128)(2,1)S(1)} %gather_fusion.1, pred[80]{0:T(512)(128)(4,1)S(1)} %compare_and_fusion), kind=kOutput, calls=%fused_computation.16 | convolution fusion | flops 677642240 | bytes 18350160 | tf_op jit(solution)/shard_map/hpi,pij->hpj/dot_general | solution.py:82
  34.1 1.5 %fusion.31 = f32[22,64,256]{2,0,1:T(8,128)S(1)} fusion(bf16[64,80,256]{2,0,1:T(8,128)(2,1)S(1)} %get-tuple-element.58, s32[80]{0:T(128)S(1)} %copy-done.9), kind=kOutput, calls=%fused_computation.46 | convolution fusion | flops 57673440 | bytes 4063552 | tf_op jit(solution)/shard_map/hpj,pw->hwj/dot_general | solution.py:33
  35.6 1.6 %fusion.119 = (bf16[64,22,256]{2,1,0:T(8,128)(2,1)S(1)}, f32[64,22,256]{2,1,0:T(8,128)S(1)}) fusion(f32[22,64,256]{2,0,1:T(8,128)S(1)} %fusion.31, bf16[64,80,256]{2,0,1:T(8,128)(2,1)S(1)} %get-tuple-element.59, s32[80]{0:T(128)S(1)} %copy-done.9), kind=kOutput, calls=%fused_computation.126 | convolution fusion | flops 58394336 | bytes 6226240 | tf_op jit(solution)/shard_map/hpj,pw->hwj/dot_general | solution.py:32
  37.3 2.5 %collective-permute-start.2 = (bf16[64,3,256]{2,1,0:T(4,128)(2,1)S(1)}, bf16[64,3,256]{2,1,0:T(4,128)(2,1)S(1)}, u32[]{:S(2)}, u32[]{:S(2)}) collective-permute-start(bf16[64,3,256]{2,1,0:T(4,128)(2,1)S(1)} %get-tuple-element.65), channel_id=1, source_target_pairs={{1,0},{2,1},{3,2},{4,3},{5,4},{6,5},{7,6},{8,7},{9,8},{10,9},{11,1... | collective-permute-start | bytes 294920 | tf_op jit(solution)/shard_map/ppermute | solution.py:26
  40.0 4.2 %collective-permute-start.3 = (bf16[64,3,256]{2,1,0:T(4,128)(2,1)S(1)}, bf16[64,3,256]{2,1,0:T(4,128)(2,1)S(1)}, u32[]{:S(2)}, u32[]{:S(2)}) collective-permute-start(bf16[64,3,256]{2,1,0:T(4,128)(2,1)S(1)} %get-tuple-element.64), channel_id=1, source_target_pairs={{0,1},{1,2},{2,3},{3,4},{4,5},{5,6},{6,7},{7,8},{8,9},{9,10},{10,1... | collective-permute-start | bytes 294920 | tf_op jit(solution)/shard_map/ppermute | solution.py:26
  44.6 1.7 %scatter-add.14 = f32[64,16,256]{2,1,0:T(8,128)S(1)} dynamic-update-slice(f32[64,16,256]{2,1,0:T(8,128)S(1)} %slice.166, f32[64,3,256]{2,1,0:T(4,128)S(1)} %slice_add_fusion.3, s32[]{:T(128)} %constant.115.clone.1, s32[]{:T(128)} %constant.116.clone.1, s32[]{:T(128)} %constant.115.clone.1) | dynamic-update-slice | bytes 393220 | tf_op jit(solution)/shard_map/scatter-add | solution.py:93
  46.4 1.7 %scatter-add.15 = f32[64,16,256]{2,1,0:T(8,128)S(1)} dynamic-update-slice(f32[64,16,256]{2,1,0:T(8,128)S(1)} %scatter-add.14, f32[64,3,256]{2,1,0:T(4,128)S(1)} %slice_add_fusion.2, s32[]{:T(128)} %constant.115.clone.1, s32[]{:T(128)} %constant.115.clone.1, s32[]{:T(128)} %constant.115.clone.1) | dynamic-update-slice | bytes 393220 | tf_op jit(solution)/shard_map/scatter-add | solution.py:94
  48.6 4.9 %collective-permute-start.4 = (bf16[64,768]{1,0:T(8,128)(2,1)S(1)}, bf16[64,768]{1,0:T(8,128)(2,1)S(1)}, u32[]{:S(2)}, u32[]{:S(2)}) collective-permute-start(bf16[64,768]{1,0:T(8,128)(2,1)S(1)} %get-tuple-element.68), channel_id=1, source_target_pairs={{0,1},{1,2},{2,3},{3,4},{4,5},{5,6},{6,7},{7,8},{8,9},{9,10},{10,1... | collective-permute-start | bytes 294920 | tf_op jit(solution)/shard_map/ppermute | solution.py:15
  53.5 1.9 %collective-permute-start.5 = (bf16[64,768]{1,0:T(8,128)(2,1)S(1)}, bf16[64,768]{1,0:T(8,128)(2,1)S(1)}, u32[]{:S(2)}, u32[]{:S(2)}) collective-permute-start(bf16[64,768]{1,0:T(8,128)(2,1)S(1)} %get-tuple-element.69), channel_id=1, source_target_pairs={{1,0},{2,1},{3,2},{4,3},{5,4},{6,5},{7,6},{8,7},{9,8},{10,9},{11,1... | collective-permute-start | bytes 294920 | tf_op jit(solution)/shard_map/ppermute | solution.py:18
  55.5 4.9 %collective-permute-done.5 = bf16[64,768]{1,0:T(8,128)(2,1)S(1)} collective-permute-done((bf16[64,768]{1,0:T(8,128)(2,1)S(1)}, bf16[64,768]{1,0:T(8,128)(2,1)S(1)}, u32[]{:S(2)}, u32[]{:S(2)}) %collective-permute-start.5) | collective-permute-done | bytes 98336 | tf_op jit(solution)/shard_map/ppermute | solution.py:18
  60.5 0.8 gather_fusion.2
  61.2 8.7 %fusion.2 = (bf16[64,80,256]{2,0,1:T(8,128)(2,1)S(1)}, bf16[64,80,256]{2,0,1:T(8,128)(2,1)}) fusion(bf16[80,256,256]{2,1,0:T(8,128)(2,1)} %param.20, bf16[80,64,256]{2,1,0:T(8,128)(2,1)S(1)} %gather_fusion.2, pred[80]{0:T(512)(128)(4,1)S(1)} %compare_and_fusion.1), kind=kOutput, calls=%fused_computation.13 | convolution fusion | flops 677642240 | bytes 18350160 | tf_op jit(solution)/shard_map/hpj,pij->hpi/dot_general | solution.py:76
  70.0 1.5 %fusion.27 = f32[16,64,256]{2,0,1:T(8,128)S(1)} fusion(bf16[64,80,256]{2,0,1:T(8,128)(2,1)S(1)} %get-tuple-element.56, s32[80]{0:T(128)S(1)} %copy-done.10), kind=kOutput, calls=%fused_computation.42 | convolution fusion | flops 41944320 | bytes 3670336 | tf_op jit(solution)/shard_map/hpi,ps->hsi/dot_general | solution.py:33
  72.0 2.6 %fusion.120 = (bf16[64,16,256]{2,1,0:T(8,128)(2,1)S(1)}, f32[64,16,256]{2,1,0:T(8,128)}) fusion(f32[64,16,256]{2,1,0:T(8,128)S(1)} %copy-done.6, f32[16,64,256]{2,0,1:T(8,128)S(1)} %fusion.27, bf16[64,80,256]{2,0,1:T(8,128)(2,1)S(1)} %copy-done.3, s32[80]{0:T(128)S(1)} %copy-done.10), kind=kOutput, calls=%fused_computation.127 | convolution fusion | flops 42730752 | bytes 6291776 | tf_op jit(solution)/shard_map/hpi,ps->hsi/dot_general | solution.py:32
  74.7 0.7 gather_fusion.3
  75.5 6.0 %fusion.1 = (bf16[64,80,256]{2,0,1:T(8,128)(2,1)S(1)}, bf16[64,80,256]{2,0,1:T(8,128)(2,1)S(1)}) fusion(bf16[80,256,256]{2,1,0:T(8,128)(2,1)} %param.20, bf16[80,64,256]{2,1,0:T(8,128)(2,1)S(1)} %gather_fusion.3, pred[80]{0:T(512)(128)(4,1)S(1)} %compare_and_fusion), kind=kOutput, calls=%fused_computation.10 | convolution fusion | flops 677642240 | bytes 18350160 | tf_op jit(solution)/shard_map/hpi,pij->hpj/dot_general | solution.py:82
  81.4 1.5 %fusion.23 = f32[22,64,256]{2,0,1:T(8,128)S(1)} fusion(bf16[64,80,256]{2,0,1:T(8,128)(2,1)S(1)} %get-tuple-element.54, s32[80]{0:T(128)S(1)} %copy-done.9), kind=kOutput, calls=%fused_computation.38 | convolution fusion | flops 57673440 | bytes 4063552 | tf_op jit(solution)/shard_map/hpj,pw->hwj/dot_general | solution.py:33
  83.0 1.6 %fusion.121 = (bf16[64,22,256]{2,1,0:T(8,128)(2,1)S(1)}, f32[64,22,256]{2,1,0:T(8,128)S(1)}) fusion(f32[22,64,256]{2,0,1:T(8,128)S(1)} %fusion.23, bf16[64,80,256]{2,0,1:T(8,128)(2,1)S(1)} %get-tuple-element.55, s32[80]{0:T(128)S(1)} %copy-done.9), kind=kOutput, calls=%fused_computation.128 | convolution fusion | flops 58394336 | bytes 6226240 | tf_op jit(solution)/shard_map/hpj,pw->hwj/dot_general | solution.py:32
  84.7 2.1 %collective-permute-start.6 = (bf16[64,3,256]{2,1,0:T(4,128)(2,1)S(1)}, bf16[64,3,256]{2,1,0:T(4,128)(2,1)S(1)}, u32[]{:S(2)}, u32[]{:S(2)}) collective-permute-start(bf16[64,3,256]{2,1,0:T(4,128)(2,1)S(1)} %get-tuple-element.63), channel_id=1, source_target_pairs={{1,0},{2,1},{3,2},{4,3},{5,4},{6,5},{7,6},{8,7},{9,8},{10,9},{11,1... | collective-permute-start | bytes 294920 | tf_op jit(solution)/shard_map/ppermute | solution.py:26
  86.7 4.8 %collective-permute-start.7 = (bf16[64,3,256]{2,1,0:T(4,128)(2,1)S(1)}, bf16[64,3,256]{2,1,0:T(4,128)(2,1)S(1)}, u32[]{:S(2)}, u32[]{:S(2)}) collective-permute-start(bf16[64,3,256]{2,1,0:T(4,128)(2,1)S(1)} %get-tuple-element.62), channel_id=1, source_target_pairs={{0,1},{1,2},{2,3},{3,4},{4,5},{5,6},{6,7},{7,8},{8,9},{9,10},{10,1... | collective-permute-start | bytes 294920 | tf_op jit(solution)/shard_map/ppermute | solution.py:26
  91.6 0.4 collective-permute-done.6
  92.0 1.7 %scatter-add.16 = f32[64,16,256]{2,1,0:T(8,128)S(1)} dynamic-update-slice(f32[64,16,256]{2,1,0:T(8,128)S(1)} %slice.173, f32[64,3,256]{2,1,0:T(4,128)S(1)} %slice_add_fusion.1, s32[]{:T(128)} %constant.115.clone.1, s32[]{:T(128)} %constant.116.clone.1, s32[]{:T(128)} %constant.115.clone.1) | dynamic-update-slice | bytes 393220 | tf_op jit(solution)/shard_map/scatter-add | solution.py:93
  93.8 1.7 %scatter-add.19 = f32[64,16,256]{2,1,0:T(8,128)S(1)} dynamic-update-slice(f32[64,16,256]{2,1,0:T(8,128)S(1)} %scatter-add.16, f32[64,3,256]{2,1,0:T(4,128)S(1)} %slice_add_fusion, s32[]{:T(128)} %constant.115.clone.1, s32[]{:T(128)} %constant.115.clone.1, s32[]{:T(128)} %constant.115.clone.1) | dynamic-update-slice | bytes 393220 | tf_op jit(solution)/shard_map/scatter-add | solution.py:94
  96.1 4.7 %collective-permute-start.8 = (bf16[64,768]{1,0:T(8,128)(2,1)S(1)}, bf16[64,768]{1,0:T(8,128)(2,1)S(1)}, u32[]{:S(2)}, u32[]{:S(2)}) collective-permute-start(bf16[64,768]{1,0:T(8,128)(2,1)S(1)} %get-tuple-element.66), channel_id=1, source_target_pairs={{0,1},{1,2},{2,3},{3,4},{4,5},{5,6},{6,7},{7,8},{8,9},{9,10},{10,1... | collective-permute-start | bytes 294920 | tf_op jit(solution)/shard_map/ppermute | solution.py:15
  100.8 1.9 %collective-permute-start.9 = (bf16[64,768]{1,0:T(8,128)(2,1)S(1)}, bf16[64,768]{1,0:T(8,128)(2,1)S(1)}, u32[]{:S(2)}, u32[]{:S(2)}) collective-permute-start(bf16[64,768]{1,0:T(8,128)(2,1)S(1)} %get-tuple-element.67), channel_id=1, source_target_pairs={{1,0},{2,1},{3,2},{4,3},{5,4},{6,5},{7,6},{8,7},{9,8},{10,9},{11,1... | collective-permute-start | bytes 294920 | tf_op jit(solution)/shard_map/ppermute | solution.py:18
  102.7 4.9 %collective-permute-done.9 = bf16[64,768]{1,0:T(8,128)(2,1)S(1)} collective-permute-done((bf16[64,768]{1,0:T(8,128)(2,1)S(1)}, bf16[64,768]{1,0:T(8,128)(2,1)S(1)}, u32[]{:S(2)}, u32[]{:S(2)}) %collective-permute-start.9) | collective-permute-done | bytes 98336 | tf_op jit(solution)/shard_map/ppermute | solution.py:18
  107.7 0.7 gather_fusion.4
  108.5 8.7 %fusion = (bf16[64,80,256]{2,0,1:T(8,128)(2,1)}, bf16[64,80,256]{2,0,1:T(8,128)(2,1)S(1)}) fusion(bf16[80,256,256]{2,1,0:T(8,128)(2,1)} %param.20, bf16[80,64,256]{2,1,0:T(8,128)(2,1)S(1)} %gather_fusion.4, pred[80]{0:T(512)(128)(4,1)S(1)} %compare_and_fusion.1), kind=kOutput, calls=%fused_computation.7 | convolution fusion | flops 677642240 | bytes 18350160 | tf_op jit(solution)/shard_map/hpj,pij->hpi/dot_general | solution.py:76
  117.3 3.3 %fusion.19 = f32[16,64,256]{2,0,1:T(8,128)S(1)} fusion(bf16[64,80,256]{2,0,1:T(8,128)(2,1)} %get-tuple-element.52, s32[80]{0:T(128)S(1)} %copy-done.10), kind=kOutput, calls=%fused_computation.34 | convolution fusion | flops 41944320 | bytes 3670336 | tf_op jit(solution)/shard_map/hpi,ps->hsi/dot_general | solution.py:33
  120.6 1.6 %fusion.75 = bf16[64,16,256]{2,1,0:T(8,128)(2,1)S(1)} fusion(f32[64,16,256]{2,1,0:T(8,128)S(1)} %copy-done.7, f32[16,64,256]{2,0,1:T(8,128)S(1)} %fusion.19, bf16[64,80,256]{2,0,1:T(8,128)(2,1)S(1)} %get-tuple-element.53, s32[80]{0:T(128)S(1)} %copy-done.10), kind=kOutput, calls=%fused_computation.74 | convolution fusion | flops 42730752 | bytes 5243200 | tf_op jit(solution)/shard_map/hpi,ps->hsi/dot_general | solution.py:32
  122.2 1.0 copy.43
  (60 shorter events, 3.5 us)
Async XLA Ops:
  2.6 11.3 %collective-permute-start = (bf16[64,768]{1,0:T(8,128)(2,1)S(1)}, bf16[64,768]{1,0:T(8,128)(2,1)S(1)}, u32[]{:S(2)}, u32[]{:S(2)}) collective-permute-start(bf16[64,768]{1,0:T(8,128)(2,1)S(1)} %get-tuple-element.70), channel_id=1, source_target_pairs={{0,1},{1,2},{2,3},{3,4},{4,5},{5,6},{6,7},{7,8},{8,9},{9,10},{10,1... | collective-permute-start | bytes 294920 | tf_op jit(solution)/shard_map/ppermute | solution.py:15
  6.3 7.6 %collective-permute-start.1 = (bf16[64,768]{1,0:T(8,128)(2,1)S(1)}, bf16[64,768]{1,0:T(8,128)(2,1)S(1)}, u32[]{:S(2)}, u32[]{:S(2)}) collective-permute-start(bf16[64,768]{1,0:T(8,128)(2,1)S(1)} %get-tuple-element.71), channel_id=1, source_target_pairs={{1,0},{2,1},{3,2},{4,3},{5,4},{6,5},{7,6},{8,7},{9,8},{10,9},{11,1... | collective-permute-start | bytes 294920 | tf_op jit(solution)/shard_map/ppermute | solution.py:18
  14.8 8.8 %copy-start.10 = (s32[80]{0:T(128)S(1)}, s32[80]{0:T(128)}, u32[]{:S(2)}) copy-start(s32[80]{0:T(128)} %param.21) | copy-start | bytes 964
  23.6 1.7 %copy-start.4 = (bf16[64,80,256]{2,0,1:T(8,128)(2,1)S(1)}, bf16[64,80,256]{2,0,1:T(8,128)(2,1)}, u32[]{:S(2)}) copy-start(bf16[64,80,256]{2,0,1:T(8,128)(2,1)} %get-tuple-element.61) | copy-start | bytes 7864324
  23.6 2.0 %copy-start.5 = (f32[64,16,256]{2,1,0:T(8,128)S(1)}, f32[64,16,256]{2,1,0:T(8,128)}, u32[]{:S(2)}) copy-start(f32[64,16,256]{2,1,0:T(8,128)} %bitcast_select_fusion) | copy-start | bytes 3145732
  28.1 6.0 %copy-start.9 = (s32[80]{0:T(128)S(1)}, s32[80]{0:T(128)}, u32[]{:S(2)}) copy-start(s32[80]{0:T(128)} %param.22) | copy-start | bytes 964
  35.6 4.2 %copy-start.11 = (s32[16]{0:T(128)S(1)}, s32[16]{0:T(128)}, u32[]{:S(2)}) copy-start(s32[16]{0:T(128)} %param.24) | copy-start | bytes 196
  35.6 4.3 %copy-start.8 = (bf16[64,4096]{1,0:T(8,128)(2,1)S(1)}, bf16[64,4096]{1,0:T(8,128)(2,1)}, u32[]{:S(2)}) copy-start(bf16[64,4096]{1,0:T(8,128)(2,1)} %param.26) | copy-start | bytes 1572868
  37.3 7.2 %collective-permute-start.2 = (bf16[64,3,256]{2,1,0:T(4,128)(2,1)S(1)}, bf16[64,3,256]{2,1,0:T(4,128)(2,1)S(1)}, u32[]{:S(2)}, u32[]{:S(2)}) collective-permute-start(bf16[64,3,256]{2,1,0:T(4,128)(2,1)S(1)} %get-tuple-element.65), channel_id=1, source_target_pairs={{1,0},{2,1},{3,2},{4,3},{5,4},{6,5},{7,6},{8,7},{9,8},{10,9},{11,1... | collective-permute-start | bytes 294920 | tf_op jit(solution)/shard_map/ppermute | solution.py:26
  40.0 8.3 %copy-start = (f32[8,8,16,256]{3,2,1,0:T(8,128)}, f32[8,8,16,256]{3,2,1,0:T(8,128)S(1)}, u32[]{:S(2)}) copy-start(f32[8,8,16,256]{3,2,1,0:T(8,128)S(1)} %copy.38) | copy-start | bytes 3145732
  40.0 6.2 %collective-permute-start.3 = (bf16[64,3,256]{2,1,0:T(4,128)(2,1)S(1)}, bf16[64,3,256]{2,1,0:T(4,128)(2,1)S(1)}, u32[]{:S(2)}, u32[]{:S(2)}) collective-permute-start(bf16[64,3,256]{2,1,0:T(4,128)(2,1)S(1)} %get-tuple-element.64), channel_id=1, source_target_pairs={{0,1},{1,2},{2,3},{3,4},{4,5},{5,6},{6,7},{7,8},{8,9},{9,10},{10,1... | collective-permute-start | bytes 294920 | tf_op jit(solution)/shard_map/ppermute | solution.py:26
  48.6 6.9 %collective-permute-start.4 = (bf16[64,768]{1,0:T(8,128)(2,1)S(1)}, bf16[64,768]{1,0:T(8,128)(2,1)S(1)}, u32[]{:S(2)}, u32[]{:S(2)}) collective-permute-start(bf16[64,768]{1,0:T(8,128)(2,1)S(1)} %get-tuple-element.68), channel_id=1, source_target_pairs={{0,1},{1,2},{2,3},{3,4},{4,5},{5,6},{6,7},{7,8},{8,9},{9,10},{10,1... | collective-permute-start | bytes 294920 | tf_op jit(solution)/shard_map/ppermute | solution.py:15
  53.5 6.8 %collective-permute-start.5 = (bf16[64,768]{1,0:T(8,128)(2,1)S(1)}, bf16[64,768]{1,0:T(8,128)(2,1)S(1)}, u32[]{:S(2)}, u32[]{:S(2)}) collective-permute-start(bf16[64,768]{1,0:T(8,128)(2,1)S(1)} %get-tuple-element.69), channel_id=1, source_target_pairs={{1,0},{2,1},{3,2},{4,3},{5,4},{6,5},{7,6},{8,7},{9,8},{10,9},{11,1... | collective-permute-start | bytes 294920 | tf_op jit(solution)/shard_map/ppermute | solution.py:18
  70.0 1.7 %copy-start.3 = (bf16[64,80,256]{2,0,1:T(8,128)(2,1)S(1)}, bf16[64,80,256]{2,0,1:T(8,128)(2,1)}, u32[]{:S(2)}) copy-start(bf16[64,80,256]{2,0,1:T(8,128)(2,1)} %get-tuple-element.57) | copy-start | bytes 7864324
  70.0 2.0 %copy-start.6 = (f32[64,16,256]{2,1,0:T(8,128)S(1)}, f32[64,16,256]{2,1,0:T(8,128)}, u32[]{:S(2)}) copy-start(f32[64,16,256]{2,1,0:T(8,128)} %bitcast_select_fusion) | copy-start | bytes 3145732
  84.5 11.0 %copy-start.1 = (f32[8,8,16,256]{3,2,1,0:T(8,128)S(1)}, f32[8,8,16,256]{3,2,1,0:T(8,128)}, u32[]{:S(2)}) copy-start(f32[8,8,16,256]{3,2,1,0:T(8,128)} %copy-done) | copy-start | bytes 3145732
  84.7 7.3 %collective-permute-start.6 = (bf16[64,3,256]{2,1,0:T(4,128)(2,1)S(1)}, bf16[64,3,256]{2,1,0:T(4,128)(2,1)S(1)}, u32[]{:S(2)}, u32[]{:S(2)}) collective-permute-start(bf16[64,3,256]{2,1,0:T(4,128)(2,1)S(1)} %get-tuple-element.63), channel_id=1, source_target_pairs={{1,0},{2,1},{3,2},{4,3},{5,4},{6,5},{7,6},{8,7},{9,8},{10,9},{11,1... | collective-permute-start | bytes 294920 | tf_op jit(solution)/shard_map/ppermute | solution.py:26
  86.7 7.0 %collective-permute-start.7 = (bf16[64,3,256]{2,1,0:T(4,128)(2,1)S(1)}, bf16[64,3,256]{2,1,0:T(4,128)(2,1)S(1)}, u32[]{:S(2)}, u32[]{:S(2)}) collective-permute-start(bf16[64,3,256]{2,1,0:T(4,128)(2,1)S(1)} %get-tuple-element.62), channel_id=1, source_target_pairs={{0,1},{1,2},{2,3},{3,4},{4,5},{5,6},{6,7},{7,8},{8,9},{9,10},{10,1... | collective-permute-start | bytes 294920 | tf_op jit(solution)/shard_map/ppermute | solution.py:26
  96.0 11.7 %copy-start.2 = (bf16[8,8,16,256]{3,1,2,0:T(8,128)(2,1)}, bf16[8,8,16,256]{3,1,2,0:T(8,128)(2,1)S(1)}, u32[]{:S(2)}) copy-start(bf16[8,8,16,256]{3,1,2,0:T(8,128)(2,1)S(1)} %copy.42) | copy-start | bytes 1572868
  96.1 6.6 %collective-permute-start.8 = (bf16[64,768]{1,0:T(8,128)(2,1)S(1)}, bf16[64,768]{1,0:T(8,128)(2,1)S(1)}, u32[]{:S(2)}, u32[]{:S(2)}) collective-permute-start(bf16[64,768]{1,0:T(8,128)(2,1)S(1)} %get-tuple-element.66), channel_id=1, source_target_pairs={{0,1},{1,2},{2,3},{3,4},{4,5},{5,6},{6,7},{7,8},{8,9},{9,10},{10,1... | collective-permute-start | bytes 294920 | tf_op jit(solution)/shard_map/ppermute | solution.py:15
  100.8 6.8 %collective-permute-start.9 = (bf16[64,768]{1,0:T(8,128)(2,1)S(1)}, bf16[64,768]{1,0:T(8,128)(2,1)S(1)}, u32[]{:S(2)}, u32[]{:S(2)}) collective-permute-start(bf16[64,768]{1,0:T(8,128)(2,1)S(1)} %get-tuple-element.67), channel_id=1, source_target_pairs={{1,0},{2,1},{3,2},{4,3},{5,4},{6,5},{7,6},{8,7},{9,8},{10,9},{11,1... | collective-permute-start | bytes 294920 | tf_op jit(solution)/shard_map/ppermute | solution.py:18
  117.3 3.3 %copy-start.7 = (f32[64,16,256]{2,1,0:T(8,128)S(1)}, f32[64,16,256]{2,1,0:T(8,128)}, u32[]{:S(2)}) copy-start(f32[64,16,256]{2,1,0:T(8,128)} %get-tuple-element.75) | copy-start | bytes 3145732
where the time goes:
time: 124 us; the launch traced here: 123 us
  matrix products  56.5 us (46%)
  starting transfers between devices  32.6 us (26%)
  local copies, waits for them, and re-layouts  16.1 us (13%)
  waiting for transfers between devices  10.3 us (8%)
  other arithmetic  6.63 us (5%)
    dot_general x3, matrix products, forward(): jnp.einsum('hpj,pij->hpi', picked, kernel, preferred_element_type=jnp.flo...  26.3 us
    ppermute x4, starting transfers between devices, passed_along(): return lax.ppermute(block, axis, route)  13.5 us
    ppermute x3, starting transfers between devices, extended(): lax.ppermute(lax.slice_in_dim(block, block.shape[dim] - width, None, axis...  13.4 us
    dot_general x2, matrix products, backward(): jnp.einsum('hpi,pij->hpj', picked, kernel, preferred_element_type=jnp.flo...  11.9 us
    ppermute x3, waiting for transfers between devices, extended(): lax.ppermute(lax.slice_in_dim(block, 0, width, axis=dim), axis, backward)  9.79 us
    dot_general x5, matrix products, pair_total(): jnp.einsum(form, low_part, selector, preferred_element_type=jnp.float32)  9.4 us
    dot_general x5, matrix products, pair_total(): jnp.einsum(form, high_part, selector, preferred_element_type=jnp.float32)  8.89 us
    ppermute x3, starting transfers between devices, extended(): lax.ppermute(lax.slice_in_dim(block, 0, width, axis=dim), axis, backward)  5.76 us
  transfers between devices with their start and end apart: 10, of which 4 were waited for; matrix products, arithmetic and copies ran while one was open for 8% of the time, Pallas kernels for 0%

commit v1 on v0

v1 whole, which is shorter than its diff:
```python
import functools

import jax
import jax.numpy as jnp
from jax import lax
from jax.experimental import pallas as pl
from jax.experimental.pallas import tpu as pltpu
from jax.sharding import PartitionSpec as P

RIM = 3
ITERS = 2
F32 = jnp.float32
BF16 = jnp.bfloat16
LANES = 128
CHUNKS = 10
UNROLL = 20
GROUP = 1024
F_TILE, F_POS, F_OWN, F_GROUP, F_MAIN, F_RIM, B_TILE, B_BLOCK, B_GROUP, B_LAST = range(10)


def divisor_below(count, most):
    return max(d for d in range(1, most + 1) if count % d == 0)


def build_table(pairs, blocks, pair_src, pair_tgt, stage, table):
    window = blocks + 2 * RIM
    stage[...] = jnp.zeros(stage.shape, jnp.int32)
    stage[0:1, 0:pairs] = pair_src[...]
    stage[1:2, 0:pairs] = pair_tgt[...]
    lane = lax.broadcasted_iota(jnp.int32, (1, LANES), 1)
    used = lane < pairs
    src, tgt = stage[0:1, :], stage[1:2, :]
    outside = (tgt < RIM) | (tgt >= RIM + blocks)
    pad = 4 * GROUP + lane
    key_f = jnp.where(used, jnp.where(outside, GROUP, 0) + src * 32 + tgt, pad).astype(F32)
    key_b = jnp.where(used, jnp.where(outside, 0, GROUP) + tgt * 32 + src, pad).astype(F32)
    place = lax.broadcasted_iota(jnp.int32, (LANES, LANES), 0).astype(F32)
    step = lax.broadcasted_iota(jnp.int32, (LANES, LANES), 1).astype(F32)

    def ordered(key):
        rows = jnp.broadcast_to(key, (LANES, LANES))
        cols = rows.T
        rank = jnp.sum(jnp.where(rows < cols, 1.0, 0.0), axis=1, keepdims=True)
        hit = rank == step
        tile = jnp.sum(jnp.where(hit, place, 0.0), axis=0, keepdims=True)
        code = jnp.sum(jnp.where(hit, cols, 0.0), axis=0, keepdims=True)
        return cols, jnp.clip(tile.astype(jnp.int32), 0, pairs - 1), code.astype(jnp.int32)

    def below(cols, limit):
        count = jnp.sum(jnp.where(cols < limit.astype(F32), 1.0, 0.0), axis=0, keepdims=True)
        return count.astype(jnp.int32)

    def last_or_zero(cols, start):
        low, high = below(cols, start), below(cols, start + 32)
        return jnp.clip(jnp.where(high > low, high - 1, pairs), 0, pairs)

    cols, tile, code = ordered(key_f)
    table[F_TILE : F_TILE + 1, :] = tile
    table[F_POS : F_POS + 1, :] = jnp.clip(code & 31, 0, window - 1)
    table[F_OWN : F_OWN + 1, :] = jnp.clip((code & 31) - RIM, 0, blocks - 1)
    table[F_GROUP : F_GROUP + 1, :] = code >> 5
    table[F_MAIN : F_MAIN + 1, :] = last_or_zero(cols, lane * 32)
    table[F_RIM : F_RIM + 1, :] = last_or_zero(cols, GROUP + lane * 32)
    cols, tile, code = ordered(key_b)
    table[B_TILE : B_TILE + 1, :] = tile
    table[B_BLOCK : B_BLOCK + 1, :] = jnp.clip(code & 31, 0, blocks - 1)
    table[B_GROUP : B_GROUP + 1, :] = code >> 5
    base = jnp.where((lane < RIM) | (lane >= RIM + blocks), 0, GROUP)
    table[B_LAST : B_LAST + 1, :] = last_or_zero(cols, base + lane * 32)


def body(
    n,
    src_cells,
    tgt_cells,
    pair_src,
    pair_tgt,
    kernel_hbm,
    src_hist_hbm,
    tgt_hist_hbm,
    warm_hbm,
    scaling_hbm,
    marginal_hbm,
    tiles,
    tiles_t,
    src_hist,
    tgt_hist,
    warm,
    scaling_out,
    marginal_out,
    stage,
    table,
    tab,
    run,
    own,
    win,
    s_bf,
    s_full,
    term_lo,
    term_hi,
    v_lo,
    v_hi,
    c_lo,
    c_hi,
    local_sem,
    tile_sem,
    send_sem,
    recv_sem,
):
    me = lax.axis_index("src")
    has_lo, has_hi = me > 0, me < n - 1
    pairs, size, _ = tiles.shape
    blocks, hists, _ = s_bf.shape
    rim_steps = RIM * (RIM + 1)
    main_steps = pairs - rim_steps
    chunk = pairs // CHUNKS

    get_warm = pltpu.make_async_copy(warm_hbm, warm, local_sem.at[0])
    get_warm.start()
    get_tiles = []
    for c in range(CHUNKS):
        part = pl.ds(c * chunk, chunk)
        copy = pltpu.make_async_copy(kernel_hbm.at[part], tiles.at[part], tile_sem.at[c])
        copy.start()
        get_tiles.append(copy)
    get_src = pltpu.make_async_copy(src_hist_hbm, src_hist, local_sem.at[1])
    get_src.start()
    get_tgt = pltpu.make_async_copy(tgt_hist_hbm, tgt_hist, local_sem.at[2])
    get_tgt.start()

    barrier = pltpu.get_barrier_semaphore()

    @pl.when(jnp.logical_not(has_lo))
    def _():
        v_lo[...] = jnp.zeros(v_lo.shape, BF16)
        c_lo[...] = jnp.zeros(c_lo.shape, BF16)

    @pl.when(jnp.logical_not(has_hi))
    def _():
        v_hi[...] = jnp.zeros(v_hi.shape, BF16)
        c_hi[...] = jnp.zeros(c_hi.shape, BF16)

    @pl.when(has_lo)
    def _():
        pl.semaphore_signal(barrier, inc=1, device_id={"src": me - 1})

    @pl.when(has_hi)
    def _():
        pl.semaphore_signal(barrier, inc=1, device_id={"src": me + 1})

    build_table(pairs, blocks, pair_src, pair_tgt, stage, table)
    get_tab = pltpu.make_async_copy(table, tab, local_sem.at[3])
    get_tab.start()

    run[pairs] = jnp.zeros((hists, size), F32)

    slot = lax.broadcasted_iota(jnp.int32, (hists, size), 1)

    def masked(ref, cells, b):
        value = ref[:, b * size : (b + 1) * size].astype(F32)
        return jnp.where(slot < cells[b], value, 0.0)

    def copies(index, to_lo, to_hi, at_hi, at_lo):
        down = pltpu.make_async_remote_copy(
            src_ref=to_lo,
            dst_ref=at_hi,
            send_sem=send_sem.at[index, 0],
            recv_sem=recv_sem.at[index, 0],
            device_id={"src": me - 1},
        )
        up = pltpu.make_async_remote_copy(
            src_ref=to_hi,
            dst_ref=at_lo,
            send_sem=send_sem.at[index, 1],
            recv_sem=recv_sem.at[index, 1],
            device_id={"src": me + 1},
        )
        return down, up

    def start(down, up):
        @pl.when(has_lo)
        def _():
            down.start()

        @pl.when(has_hi)
        def _():
            up.start()

    def receive(down, up):
        @pl.when(has_hi)
        def _():
            down.wait_recv()

        @pl.when(has_lo)
        def _():
            up.wait_recv()

    def sent(down, up):
        @pl.when(has_lo)
        def _():
            down.wait_send()

        @pl.when(has_hi)
        def _():
            up.wait_send()

    def steps(low, count, tile_row, field_row, group_row, field, weights, carry):
        unroll = divisor_below(count, UNROLL)

        def some(block, carry):
            acc, before = carry
            for u in range(unroll):
                s = low + block * unroll + u
                group = tab[group_row, s]
                product = jnp.dot(
                    field[tab[field_row, s]],
                    weights[tab[tile_row, s]],
                    preferred_element_type=F32,
                )
                acc = jnp.where(group == before, acc, 0.0) + product
                before = group
                run[s] = acc
            return acc, before

        return lax.fori_loop(0, count // unroll, some, carry)

    def fresh():
        return jnp.zeros((hists, size), F32), jnp.int32(-1)

    edges = list(range(RIM)) + list(range(blocks - RIM, blocks))
    inner = list(range(RIM, blocks - RIM))
    pending = []

    def send_field(k):
        pair = copies(
            k,
            own.at[k, pl.ds(0, RIM)],
            own.at[k, pl.ds(blocks - RIM, RIM)],
            v_hi.at[k],
            v_lo.at[k],
        )
        start(*pair)
        pending.append(pair)
        return pair

    def put_field(k, b, value):
        rounded = value.astype(BF16)
        own[k, b] = rounded
        win[RIM + b] = rounded

    def forward(k, pair):
        carry = steps(0, main_steps, F_TILE, F_OWN, F_GROUP, own.at[k], tiles_t, fresh())
        receive(*pair)
        for r in range(RIM):
            win[r] = v_lo[k, r]
            win[RIM + blocks + r] = v_hi[k, r]
        steps(main_steps, rim_steps, F_TILE, F_POS, F_GROUP, win, tiles_t, carry)

    def image(b):
        return run[tab[F_MAIN, b]] + run[tab[F_RIM, b]]

    get_warm.wait()
    for b in edges:
        put_field(0, b, masked(warm, tgt_cells, b))

    pl.semaphore_wait(barrier, has_lo.astype(jnp.int32) + has_hi.astype(jnp.int32))

    pair = send_field(0)
    for b in inner:
        put_field(0, b, masked(warm, tgt_cells, b))

    for c in range(CHUNKS):
        get_tiles[c].wait()

        def turn(i, carry, c=c):
            tiles_t[c * chunk + i] = tiles[c * chunk + i].T
            return carry

        lax.fori_loop(0, chunk, turn, 0, unroll=divisor_below(chunk, 4))
    get_tab.wait()
    get_src.wait()
    get_tgt.wait()

    put_scaling = pltpu.make_async_copy(scaling_out, scaling_hbm, local_sem.at[4])
    for k in range(ITERS):
        forward(k, pair)
        for b in range(blocks):
            scale = masked(src_hist, src_cells, b) / image(b)
            s_bf[b] = scale.astype(BF16)
            if k == ITERS - 1:
                s_full[b] = scale
        carry = steps(0, rim_steps, B_TILE, B_BLOCK, B_GROUP, s_bf, tiles, fresh())
        for r in range(RIM):
            term_lo[k, r] = run[tab[B_LAST, r]].astype(BF16)
            term_hi[k, r] = run[tab[B_LAST, RIM + blocks + r]].astype(BF16)
        terms = copies(ITERS + 1 + k, term_lo.at[k], term_hi.at[k], c_hi.at[k], c_lo.at[k])
        start(*terms)
        pending.append(terms)
        steps(rim_steps, main_steps, B_TILE, B_BLOCK, B_GROUP, s_bf, tiles, carry)
        receive(*terms)

        def finish(b):
            total = run[tab[B_LAST, RIM + b]]
            if b < RIM:
                total = total + c_lo[k, b].astype(F32)
            if b >= blocks - RIM:
                total = total + c_hi[k, b - (blocks - RIM)].astype(F32)
            value = masked(tgt_hist, tgt_cells, b) / total
            put_field(k + 1, b, value)
            if k == ITERS - 1:
                scaling_out[:, b * size : (b + 1) * size] = value.astype(BF16)

        for b in edges:
            finish(b)
        pair = send_field(k + 1)
        for b in inner:
            finish(b)
    put_scaling.start()
    forward(ITERS, pair)
    for b in range(blocks):
        marginal_out[:, b * size : (b + 1) * size] = (s_full[b] * image(b)).astype(BF16)
    put_marginal = pltpu.make_async_copy(marginal_out, marginal_hbm, local_sem.at[5])
    put_marginal.start()
    for pair in pending:
        sent(*pair)
    put_scaling.wait()
    put_marginal.wait()


def local(
    kernel,
    pair_source,
    pair_target,
    source_cells,
    target_cells,
    source_hist,
    target_hist,
    warm_start,
):
    pairs, size, _ = kernel.shape
    blocks = source_cells.shape[0]
    hists = source_hist.shape[0]
    window = blocks + 2 * RIM
    n = lax.axis_size("src")
    exchanges = 2 * ITERS + 1
    flat = source_hist.shape
    smem = pl.BlockSpec(memory_space=pltpu.SMEM)
    vmem = pl.BlockSpec(memory_space=pltpu.VMEM)
    hbm = pl.BlockSpec(memory_space=pl.ANY)
    field = (blocks, hists, size)
    rim = (RIM, hists, size)
    return pl.pallas_call(
        functools.partial(body, n),
        out_shape=(jax.ShapeDtypeStruct(flat, BF16), jax.ShapeDtypeStruct(flat, BF16)),
        in_specs=[smem, smem, vmem, vmem, hbm, hbm, hbm, hbm],
        out_specs=(hbm, hbm),
        scratch_shapes=[
            pltpu.VMEM(kernel.shape, BF16),
            pltpu.VMEM(kernel.shape, BF16),
            pltpu.VMEM(flat, BF16),
            pltpu.VMEM(flat, BF16),
            pltpu.VMEM(flat, BF16),
            pltpu.VMEM(flat, BF16),
            pltpu.VMEM(flat, BF16),
            pltpu.VMEM((8, LANES), jnp.int32),
            pltpu.VMEM((16, LANES), jnp.int32),
            pltpu.SMEM((16, LANES), jnp.int32),
            pltpu.VMEM((pairs + 1, hists, size), F32),
            pltpu.VMEM((ITERS + 1,) + field, BF16),
            pltpu.VMEM((window, hists, size), BF16),
            pltpu.VMEM(field, BF16),
            pltpu.VMEM(field, F32),
            pltpu.VMEM((ITERS,) + rim, BF16),
            pltpu.VMEM((ITERS,) + rim, BF16),
            pltpu.VMEM((ITERS + 1,) + rim, BF16),
            pltpu.VMEM((ITERS + 1,) + rim, BF16),
            pltpu.VMEM((ITERS,) + rim, BF16),
            pltpu.VMEM((ITERS,) + rim, BF16),
            pltpu.SemaphoreType.DMA((6,)),
            pltpu.SemaphoreType.DMA((CHUNKS,)),
            pltpu.SemaphoreType.DMA((exchanges, 2)),
            pltpu.SemaphoreType.DMA((exchanges, 2)),
        ],
        compiler_params=pltpu.CompilerParams(
            collective_id=0, has_side_effects=True, vmem_limit_bytes=52 * 2**20
        ),
    )(
        source_cells,
        target_cells,
        pair_source.reshape(1, pairs),
        pair_target.reshape(1, pairs),
        kernel,
        source_hist,
        target_hist,
        warm_start,
    )


def solution(mesh):
    in_specs = (
        P(("grp", "src"), None, None),
        P(("grp", "src")),
        P(("grp", "src")),
        P(("grp", "src")),
        P(("grp", "src")),
        P(None, ("grp", "src")),
        P(None, ("grp", "src")),
        P(None, ("grp", "src")),
    )
    out_specs = (P(None, ("grp", "src")), P(None, ("grp", "src")))
    return jax.shard_map(local, mesh=mesh, in_specs=in_specs, out_specs=out_specs, check_vma=False)
```

time: 124 us -> 34.7 us (0.28)
  matrix products: 56.5 us -> 0 us
  starting transfers between devices: 32.6 us -> 0 us
  Pallas kernels: 0 us -> 28.4 us
  local copies, waits for them, and re-layouts: 16.1 us -> 5.24 us
  waiting for transfers between devices: 10.3 us -> 0 us
  other arithmetic: 6.63 us -> 0 us
    dot_general x15 -> x0, matrix products: 56.5 us -> none  [the longest x3 26.3 us: forward(): jnp.einsum('hpj,pij->hpi', picked, kernel, preferred_element_type=jnp.flo...]
    ppermute x10 -> x0, starting transfers between devices: 32.6 us -> none  [the longest x4 13.5 us: passed_along(): return lax.ppermute(block, axis, route)]
    pallas_call x0 -> x1, Pallas kernels: none -> 28.4 us  [local(): pl.pallas_call(functools.partial(body, n), out_shape=(jax.ShapeDtypeStruc...]
    ppermute x10 -> x0, waiting for transfers between devices: 10.3 us -> none  [the longest x3 9.79 us: extended(): lax.ppermute(lax.slice_in_dim(block, 0, width, axis=dim), axis, backward)]
    scatter-add x4 -> x0, local copies, waits for them, and re-layouts: 6.84 us -> none  [the longest x2 3.48 us: backward(): own_part = own_part.at[:, :reach].add(from_lower)]
    gather x5 -> x0, local copies, waits for them, and re-layouts: 3.74 us -> none  [the longest x3 2.25 us: forward(): picked = jnp.take(window, window_pos, axis=1)]
    select_n x3 -> x0, other arithmetic: 2.41 us -> none  [the longest x1 1.1 us: masked(): jnp.where(live[None], field.reshape(hist_count, block_count, block_len).a...]
    convert_element_type x3 -> x0, other arithmetic: 1.66 us -> none  [the longest x2 1.4 us: forward(): field.astype(jnp.bfloat16).reshape(hist_count, block_count * block_len)]
  transfers between devices with their start and end apart: 10 -> 0, of which waited for: 4 -> 0; matrix products, arithmetic and copies ran while one was open for 8% -> 0% of each run, Pallas kernels for 0% -> 0%
where the time goes in v1:
time: 34.7 us; the launch traced here: 34.3 us
  Pallas kernels  28.4 us (82%)
  local copies, waits for them, and re-layouts  5.24 us (15%)
  between operations  0.65 us (2%)
    pallas_call x1, Pallas kernels, local(): pl.pallas_call(functools.partial(body, n), out_shape=(jax.ShapeDtypeStruc...  28.4 us
    unnamed x12, local copies, waits for them, and re-layouts  5.24 us

profile of v1, /device:TPU:19, one launch (start us, length us, event | category | flops | bytes accessed | tf_op | source)
XLA Modules:
  0.0 34.3 jit_solution(10739250651963028830)
XLA Ops:
  0.6 0.0 copy-start
  0.6 1.0 %copy-done = bf16[64,4096]{1,0:T(8,128)(2,1)S(1)} copy-done((bf16[64,4096]{1,0:T(8,128)(2,1)S(1)}, bf16[64,4096]{1,0:T(8,128)(2,1)}, u32[]{:S(2)}) %copy-start) | copy-done | bytes 524312
  1.7 0.0 copy-start.1
  1.7 0.7 %copy-done.1 = s32[16]{0:T(128)S(1)} copy-done((s32[16]{0:T(128)S(1)}, s32[16]{0:T(128)}, u32[]{:S(2)}) %copy-start.1) | copy-done | bytes 88
  2.3 0.0 copy-start.2
  2.3 0.7 %copy-done.2 = s32[16]{0:T(128)S(1)} copy-done((s32[16]{0:T(128)S(1)}, s32[16]{0:T(128)}, u32[]{:S(2)}) %copy-start.2) | copy-done | bytes 88
  3.0 0.0 copy-start.3
  3.0 0.7 %copy-done.3 = s32[80]{0:T(128)S(1)} copy-done((s32[80]{0:T(128)S(1)}, s32[80]{0:T(128)}, u32[]{:S(2)}) %copy-start.3) | copy-done | bytes 344
  3.6 0.0 copy-start.4
  3.6 0.7 %copy-done.4 = s32[80]{0:T(128)S(1)} copy-done((s32[80]{0:T(128)S(1)}, s32[80]{0:T(128)}, u32[]{:S(2)}) %copy-start.4) | copy-done | bytes 344
  4.3 28.4 %shard_map.95 = (bf16[64,4096]{1,0:T(8,128)(2,1)S(1)}, bf16[64,4096]{1,0:T(8,128)(2,1)S(1)}) custom-call(s32[16]{0:T(128)S(1)} %copy-done.1, s32[16]{0:T(128)S(1)} %copy-done.2, s32[1,80]{1,0:T(1,128)S(1)} %bitcast.2, s32[1,80]{1,0:T(1,128)S(1)} %bitcast.3, bf16[80,256,256]{2,1,0:T(8,128)(2,1)} %kernel_hbm.1, bf16[64,4096]{1,0:T(8,128)(2,1)S(1)} %copy-done, ...), custom_call_target="tpu_custom_call" | custom-call | tf_op jit(solution)/shard_map/pallas_call | solution.py:352
  32.7 0.8 %copy.12 = bf16[64,4096]{1,0:T(8,128)(2,1)} copy(bf16[64,4096]{1,0:T(8,128)(2,1)S(1)} %get-tuple-element.4) | data formatting | bytes 1048576
  33.5 0.8 %copy.13 = bf16[64,4096]{1,0:T(8,128)(2,1)} copy(bf16[64,4096]{1,0:T(8,128)(2,1)S(1)} %get-tuple-element.5) | data formatting | bytes 1048576
Async XLA Ops:
  0.6 1.0 %copy-start = (bf16[64,4096]{1,0:T(8,128)(2,1)S(1)}, bf16[64,4096]{1,0:T(8,128)(2,1)}, u32[]{:S(2)}) copy-start(bf16[64,4096]{1,0:T(8,128)(2,1)} %src_hist_hbm.1) | copy-start | bytes 1572868
  1.7 0.7 %copy-start.1 = (s32[16]{0:T(128)S(1)}, s32[16]{0:T(128)}, u32[]{:S(2)}) copy-start(s32[16]{0:T(128)} %src_cells.1) | copy-start | bytes 196
  2.3 0.7 %copy-start.2 = (s32[16]{0:T(128)S(1)}, s32[16]{0:T(128)}, u32[]{:S(2)}) copy-start(s32[16]{0:T(128)} %tgt_cells.1) | copy-start | bytes 196
  3.0 0.7 %copy-start.3 = (s32[80]{0:T(128)S(1)}, s32[80]{0:T(128)}, u32[]{:S(2)}) copy-start(s32[80]{0:T(128)} %param.9) | copy-start | bytes 964
  3.6 0.7 %copy-start.4 = (s32[80]{0:T(128)S(1)}, s32[80]{0:T(128)}, u32[]{:S(2)}) copy-start(s32[80]{0:T(128)} %param.10) | copy-start | bytes 964

commit v2 on v1

--- a/solution.py
+++ b/solution.py
@@ -13,7 +13,7 @@
 BF16 = jnp.bfloat16
 LANES = 128
 CHUNKS = 10
-UNROLL = 20
+UNROLL = 34
 GROUP = 1024
 F_TILE, F_POS, F_OWN, F_GROUP, F_MAIN, F_RIM, B_TILE, B_BLOCK, B_GROUP, B_LAST = range(10)
 
@@ -71,16 +71,20 @@
 
 def body(
     n,
-    src_cells,
-    tgt_cells,
-    pair_src,
-    pair_tgt,
+    src_cells_hbm,
+    tgt_cells_hbm,
+    pair_src_hbm,
+    pair_tgt_hbm,
     kernel_hbm,
     src_hist_hbm,
     tgt_hist_hbm,
     warm_hbm,
     scaling_hbm,
     marginal_hbm,
+    src_cells,
+    tgt_cells,
+    pair_src,
+    pair_tgt,
     tiles,
     tiles_t,
     src_hist,
@@ -115,6 +119,18 @@
     main_steps = pairs - rim_steps
     chunk = pairs // CHUNKS
 
+    small = []
+    for i, (ref, held) in enumerate(
+        (
+            (pair_src_hbm, pair_src),
+            (pair_tgt_hbm, pair_tgt),
+            (tgt_cells_hbm, tgt_cells),
+            (src_cells_hbm, src_cells),
+        )
+    ):
+        copy = pltpu.make_async_copy(ref, held, local_sem.at[6 + i])
+        copy.start()
+        small.append(copy)
     get_warm = pltpu.make_async_copy(warm_hbm, warm, local_sem.at[0])
     get_warm.start()
     get_tiles = []
@@ -148,6 +164,8 @@
     def _():
         pl.semaphore_signal(barrier, inc=1, device_id={"src": me + 1})
 
+    small[0].wait()
+    small[1].wait()
     build_table(pairs, blocks, pair_src, pair_tgt, stage, table)
     get_tab = pltpu.make_async_copy(table, tab, local_sem.at[3])
     get_tab.start()
@@ -204,7 +222,7 @@
         def _():
             up.wait_send()
 
-    def steps(low, count, tile_row, field_row, group_row, field, weights, carry):
+    def steps(low, count, tile_row, field_row, group_row, field, carry, turning=False):
         unroll = divisor_below(count, UNROLL)
 
         def some(block, carry):
@@ -212,9 +230,16 @@
             for u in range(unroll):
                 s = low + block * unroll + u
                 group = tab[group_row, s]
+                if turning:
+                    tile = tiles[tab[tile_row, s]].T
+                    tiles_t[s] = tile
+                elif tile_row == F_TILE:
+                    tile = tiles_t[s]
+                else:
+                    tile = tiles[tab[tile_row, s]]
                 product = jnp.dot(
                     field[tab[field_row, s]],
-                    weights[tab[tile_row, s]],
+                    tile,
                     preferred_element_type=F32,
                 )
                 acc = jnp.where(group == before, acc, 0.0) + product
@@ -249,17 +274,19 @@
         win[RIM + b] = rounded
 
     def forward(k, pair):
-        carry = steps(0, main_steps, F_TILE, F_OWN, F_GROUP, own.at[k], tiles_t, fresh())
+        carry = steps(0, main_steps, F_TILE, F_OWN, F_GROUP, own.at[k], fresh(), k == 0)
         receive(*pair)
         for r in range(RIM):
             win[r] = v_lo[k, r]
             win[RIM + blocks + r] = v_hi[k, r]
-        steps(main_steps, rim_steps, F_TILE, F_POS, F_GROUP, win, tiles_t, carry)
+        steps(main_steps, rim_steps, F_TILE, F_POS, F_GROUP, win, carry, k == 0)
 
     def image(b):
         return run[tab[F_MAIN, b]] + run[tab[F_RIM, b]]
 
     get_warm.wait()
+    small[2].wait()
+    small[3].wait()
     for b in edges:
         put_field(0, b, masked(warm, tgt_cells, b))
 
@@ -271,12 +298,6 @@
 
     for c in range(CHUNKS):
         get_tiles[c].wait()
-
-        def turn(i, carry, c=c):
-            tiles_t[c * chunk + i] = tiles[c * chunk + i].T
-            return carry
-
-        lax.fori_loop(0, chunk, turn, 0, unroll=divisor_below(chunk, 4))
     get_tab.wait()
     get_src.wait()
     get_tgt.wait()
@@ -289,14 +310,14 @@
             s_bf[b] = scale.astype(BF16)
             if k == ITERS - 1:
                 s_full[b] = scale
-        carry = steps(0, rim_steps, B_TILE, B_BLOCK, B_GROUP, s_bf, tiles, fresh())
+        carry = steps(0, rim_steps, B_TILE, B_BLOCK, B_GROUP, s_bf, fresh())
         for r in range(RIM):
             term_lo[k, r] = run[tab[B_LAST, r]].astype(BF16)
             term_hi[k, r] = run[tab[B_LAST, RIM + blocks + r]].astype(BF16)
         terms = copies(ITERS + 1 + k, term_lo.at[k], term_hi.at[k], c_hi.at[k], c_lo.at[k])
         start(*terms)
         pending.append(terms)
-        steps(rim_steps, main_steps, B_TILE, B_BLOCK, B_GROUP, s_bf, tiles, carry)
+        steps(rim_steps, main_steps, B_TILE, B_BLOCK, B_GROUP, s_bf, carry)
         receive(*terms)
 
         def finish(b):
@@ -344,17 +365,19 @@
     n = lax.axis_size("src")
     exchanges = 2 * ITERS + 1
     flat = source_hist.shape
-    smem = pl.BlockSpec(memory_space=pltpu.SMEM)
-    vmem = pl.BlockSpec(memory_space=pltpu.VMEM)
     hbm = pl.BlockSpec(memory_space=pl.ANY)
     field = (blocks, hists, size)
     rim = (RIM, hists, size)
     return pl.pallas_call(
         functools.partial(body, n),
         out_shape=(jax.ShapeDtypeStruct(flat, BF16), jax.ShapeDtypeStruct(flat, BF16)),
-        in_specs=[smem, smem, vmem, vmem, hbm, hbm, hbm, hbm],
+        in_specs=[hbm] * 8,
         out_specs=(hbm, hbm),
         scratch_shapes=[
+            pltpu.SMEM(source_cells.shape, jnp.int32),
+            pltpu.SMEM(target_cells.shape, jnp.int32),
+            pltpu.VMEM((1, pairs), jnp.int32),
+            pltpu.VMEM((1, pairs), jnp.int32),
             pltpu.VMEM(kernel.shape, BF16),
             pltpu.VMEM(kernel.shape, BF16),
             pltpu.VMEM(flat, BF16),
@@ -376,13 +399,13 @@
             pltpu.VMEM((ITERS + 1,) + rim, BF16),
             pltpu.VMEM((ITERS,) + rim, BF16),
             pltpu.VMEM((ITERS,) + rim, BF16),
-            pltpu.SemaphoreType.DMA((6,)),
+            pltpu.SemaphoreType.DMA((10,)),
             pltpu.SemaphoreType.DMA((CHUNKS,)),
             pltpu.SemaphoreType.DMA((exchanges, 2)),
             pltpu.SemaphoreType.DMA((exchanges, 2)),
         ],
         compiler_params=pltpu.CompilerParams(
-            collective_id=0, has_side_effects=True, vmem_limit_bytes=52 * 2**20
+            collective_id=0, has_side_effects=True, vmem_limit_bytes=62 * 2**20
         ),
     )(
         source_cells,

time: 34.7 us -> 31 us (0.89)
  Pallas kernels: 28.4 us -> 26.3 us
  local copies, waits for them, and re-layouts: 5.24 us -> 3.74 us
    pallas_call x1, Pallas kernels: 28.4 us -> 26.3 us  [local(): pl.pallas_call(functools.partial(body, n), out_shape=(jax.ShapeDtypeStruc...]
    unnamed x12 -> x2, local copies, waits for them, and re-layouts: 5.24 us -> 3.74 us
where the time goes in v2:
time: 31 us; the launch traced here: 30.7 us
  Pallas kernels  26.3 us (85%)
  local copies, waits for them, and re-layouts  3.74 us (12%)
  between operations  0.64 us (2%)
    pallas_call x1, Pallas kernels, local(): pl.pallas_call(functools.partial(body, n), out_shape=(jax.ShapeDtypeStruc...  26.3 us
    unnamed x2, local copies, waits for them, and re-layouts  3.74 us

profile of v2, /device:TPU:19, one launch (start us, length us, event | category | flops | bytes accessed | tf_op | source)
XLA Modules:
  0.0 30.7 jit_solution(9985955564023339844)
XLA Ops:
  0.6 26.3 %shard_map.95 = (bf16[64,4096]{1,0:T(8,128)(2,1)}, bf16[64,4096]{1,0:T(8,128)(2,1)}) custom-call(s32[16]{0:T(128)} %src_cells_hbm.1, s32[16]{0:T(128)} %tgt_cells_hbm.1, s32[1,80]{1,0:T(1,128)} %bitcast.2, s32[1,80]{1,0:T(1,128)} %bitcast.3, bf16[80,256,256]{2,1,0:T(8,128)(2,1)} %kernel_hbm.1, bf16[64,4096]{1,0:T(8,128)(2,1)} %src_hist_hbm.1, ...), custom_call_target="tpu_custom_call" | custom-call | tf_op jit(solution)/shard_map/pallas_call | solution.py:371
  27.0 1.9 %copy.12 = bf16[64,4096]{1,0:T(8,128)(2,1)} copy(bf16[64,4096]{1,0:T(8,128)(2,1)} %get-tuple-element.4) | data formatting | bytes 1048576
  28.8 1.9 %copy.13 = bf16[64,4096]{1,0:T(8,128)(2,1)} copy(bf16[64,4096]{1,0:T(8,128)(2,1)} %get-tuple-element.5) | data formatting | bytes 1048576
